TPU v7x, 128 devices: a whole 4x4x4 slice. The times are simulated.
128 devices in a mesh: team: 16 (over x_hi, z, core), tile: 8 (over y, x_lo).
Axes of the slice: x: 4 (x_hi: 2, x_lo: 2; x = x_hi * 2 + x_lo), y: 4, z: 4, core: 2. Of those that a mesh axis runs over, the one named last changes fastest.
Arguments:
- points: float32 [8, 131072], P(None, ('team', 'tile')), may hold values from -6 to 6
- scales: float32 [8], replicated, may hold values from 1.2 to 3
- vectors: float32 [16, 131072], P(None, ('team', 'tile')), may hold values from -6 to 6
- plan: int32 [2], replicated, may hold values from 1 to 15, as said below
Outputs:
- smoothed: float32 [16, 131072], P(None, ('team', 'tile'))
Inputs may be any that keep to these rules, and one draw needn't show every extreme that they name: `plan`: the 2 values are distinct; one of them is 15.
All inputs are finite; a program needn't handle non-finite values.
Results may differ from a plain program's by a relative error of at most 0.00084.
Values sent between devices are 32-bit elements; how exact they have to be, the bound alone decides.
A program may use at most 64 MiB of HBM per device.

v0:
```python
import functools
import math

import jax
import jax.numpy as jnp
from jax import lax
from jax.experimental import pallas as pl
from jax.experimental.pallas import tpu as pltpu
from jax.sharding import PartitionSpec as P

MESH = pl.DeviceIdType.MESH
VMEM = pltpu.VMEM
F32 = jnp.float32
BF16 = jnp.bfloat16

SHRINK = math.sqrt(0.05)
RATE = -10.0 / math.log(2.0)
COORDS = 8
RHS = 16
DEPTH = 64
UNIT = 512
HOPS = 4
PER_ROW = 17


def tile_id(offset):
    count = lax.axis_size("tile")
    return {"tile": lax.rem(lax.axis_index("tile") + offset + count, count)}


def team_id(pairing):
    me = lax.axis_index("team")
    bits = lax.axis_size("team").bit_length() - 1
    other = me * 0
    for bit in range(bits):
        mine = lax.rem(me // (1 << bit), 2)
        other = other + (1 << bit) * (1 - mine if pairing >> bit & 1 else mine)
    return {"team": other}


def greet():
    barrier = pltpu.get_barrier_semaphore()
    tiles = lax.axis_size("tile")
    teams = lax.axis_size("team")
    friends = [tile_id(step) for step in range(1, tiles)]
    friends += [team_id(1 << bit) for bit in range(teams.bit_length() - 1)]
    friends.append(team_id(teams - 1))
    for friend in friends:
        pl.semaphore_signal(barrier, inc=1, device_id=friend, device_id_type=MESH)
    pl.semaphore_wait(barrier, len(friends))


def remote(src, dst, send, recv, target):
    return pltpu.make_async_remote_copy(
        src_ref=src, dst_ref=dst, send_sem=send, recv_sem=recv, device_id=target, device_id_type=MESH
    )


def chosen(plan_ref, bit, arrived, held):
    pairing = plan_ref[0] + plan_ref[1] - 15
    taken = jnp.bitwise_and(jnp.right_shift(pairing, bit), 1).astype(F32)
    mask = jnp.full(held.shape, taken, F32) > 0.5
    return jnp.where(mask, arrived, held)


def fetch_kernel(plan_ref, own_ref, cols_ref, far_ref, near_ref, held, got, sends, recvs):
    greet()
    copies = []
    for hop in range(1, HOPS + 1):
        copies.append(remote(own_ref, cols_ref.at[hop - 1], sends.at[hop - 1], recvs.at[hop - 1], tile_id(-hop)))
    copies.append(remote(own_ref, far_ref, sends.at[4], recvs.at[4], team_id(15)))
    for copy in copies:
        copy.start()
    for bit in range(4):
        src = own_ref if bit == 0 else held.at[bit - 1]
        copy = remote(src, got.at[bit], sends.at[5 + bit], recvs.at[5 + bit], team_id(1 << bit))
        copy.start()
        copy.wait()
        value = chosen(plan_ref, bit, got[bit], src[...])
        if bit < 3:
            held[bit] = value
        else:
            near_ref[...] = value
    for copy in copies:
        copy.wait()


def give_kernel(plan_ref, vec_ref, rows_ref, cols_ref, out_ref, back, far, held, got, sends, recvs):
    greet()
    size = vec_ref.shape[1]
    copies = []
    for hop in range(1, HOPS + 1):
        src = cols_ref.at[hop]
        copies.append(remote(src, back.at[hop - 1], sends.at[hop - 1], recvs.at[hop - 1], tile_id(hop)))
    copies.append(remote(rows_ref.at[1], far, sends.at[4], recvs.at[4], team_id(15)))
    for copy in copies:
        copy.start()
    total = 0.5 * vec_ref[...] + rows_ref[0] + cols_ref[0]
    for bit in range(4):
        src = rows_ref.at[2] if bit == 0 else held.at[bit - 1]
        copy = remote(src, got.at[bit], sends.at[5 + bit], recvs.at[5 + bit], team_id(1 << bit))
        copy.start()
        copy.wait()
        value = chosen(plan_ref, bit, got[bit], src[...])
        if bit < 3:
            held[bit] = value
        else:
            total = total + value
    for copy in copies:
        copy.wait()
    total = total + far[...]
    for hop in range(HOPS):
        total = total + back[hop]
    out_ref[...] = total


def pieces(value, count):
    out = []
    for _ in range(count):
        piece = value.astype(BF16).astype(F32)
        out.append(piece)
        value = value - piece
    return out


def split(shard, scales):
    scaled = shard[:COORDS] / scales * SHRINK
    one, two, three = pieces(scaled, 3)
    norm = jnp.sum(scaled * scaled, axis=0, keepdims=True)
    return one, two, three, pieces(norm, 3)


def place(parts, size):
    row = lax.broadcasted_iota(jnp.int32, (8, size), 0)
    out = jnp.zeros((8, size), F32)
    for at, part in enumerate(parts):
        out = jnp.where(row == at, part, out)
    return out


def col_operand(shard, scales):
    one, two, three, norms = split(shard, scales)
    unit = jnp.ones_like(norms[0])
    tail = place(norms + [unit] * 3, shard.shape[1])
    return jnp.concatenate([one, one, one, two, two, three, tail, jnp.zeros_like(tail)], 0).astype(BF16)


def row_operand(shard, scales):
    one, two, three, norms = split(shard, scales)
    unit = jnp.ones_like(norms[0])
    tail = place([unit] * 3 + norms, shard.shape[1])
    stack = [-2.0 * one, -2.0 * two, -2.0 * three, -2.0 * one, -2.0 * two, -2.0 * one, tail]
    stack += [jnp.zeros_like(tail)] * 9
    return jnp.concatenate(stack, 0).T


def matern(small):
    small = jnp.maximum(small, 1e-30)
    w = small * lax.rsqrt(small)
    return ((w * (w + 0.3) + 0.03) * jnp.exp2(w * RATE)).astype(BF16)


def pair_kernel(
    scales_ref, own_ref, cols_ref, far_ref, near_ref, rows_out, cols_out, small, work, col_x, col_v, row_v, acc_r, acc_c
):
    size = own_ref.shape[1]
    halves = size // UNIT
    units = 3 * PER_ROW
    scales = scales_ref[...]
    for row, ref in enumerate((own_ref, far_ref, near_ref)):
        shard = ref[...]
        work[2 * UNIT + row * size : 2 * UNIT + (row + 1) * size, 0:128] = row_operand(shard, scales).astype(BF16)
        row_v[:, row * size : (row + 1) * size] = shard[COORDS:].astype(BF16)
    for hop in range(HOPS + 1):
        shard = own_ref[...] if hop == 0 else cols_ref[hop - 1]
        col_x[:, hop * size : (hop + 1) * size] = col_operand(shard, scales)
        col_v[:, hop * size : (hop + 1) * size] = shard[COORDS:].astype(BF16)
    acc_r[...] = jnp.zeros_like(acc_r)
    acc_c[...] = jnp.zeros_like(acc_c)
    upper = (lax.axis_index("tile") >= lax.axis_size("tile") // 2).astype(jnp.int32)

    def where(unit):
        shard, item = unit // PER_ROW, lax.rem(unit, PER_ROW)
        inner = item - 3
        row = jnp.where(item < 3, (item == 1).astype(jnp.int32), lax.rem(inner // 2, 2))
        row = jnp.where(item == 15, upper, jnp.where(item == 16, 1, row))
        col = jnp.where(item < 3, (item > 0).astype(jnp.int32), 2 * (1 + inner // 4) + lax.rem(inner, 2))
        col = jnp.where(item == 15, 8, jnp.where(item == 16, 8 + upper, col))
        one_way = (item < 2).astype(F32)
        return pl.multiple_of((shard * halves + row) * UNIT, UNIT), pl.multiple_of(col * UNIT, UNIT), 1.0 - one_way

    chunk = 256

    def distances(row, col, at):
        rows = work[pl.ds(pl.multiple_of(2 * UNIT + row + at, chunk), chunk), 0:DEPTH]
        return jnp.dot(rows, col_x[:, pl.ds(col, UNIT)], preferred_element_type=F32)

    def products(base, row, col, both, at):
        part = work[pl.ds(pl.multiple_of(base + at, chunk), chunk), :]
        rows = pl.ds(pl.multiple_of(row + at, chunk), chunk)
        cols = pl.ds(col, UNIT)
        acc_c[:, cols] += jnp.dot(row_v[:, rows], part, preferred_element_type=F32)
        acc_r[:, rows] += both * lax.dot_general(
            col_v[:, cols], part, (((1,), (1,)), ((), ())), preferred_element_type=F32
        )

    def step(unit, carry):
        base = pl.multiple_of(lax.rem(unit, 2) * UNIT, UNIT)
        last = pl.multiple_of(UNIT - base, UNIT)
        next_row, next_col, _ = where(jnp.minimum(unit + 1, units - 1))
        last_row, last_col, both = where(jnp.maximum(unit - 1, 0))
        for at in range(0, UNIT, chunk):
            fresh = distances(next_row, next_col, at)
            products(last, last_row, last_col, both, at)
            for line in range(at, at + chunk, 16):
                work[pl.ds(pl.multiple_of(base + line, 16), 16), :] = matern(small[line : line + 16, :])
            small[at : at + chunk, :] = fresh
        return carry

    first_row, first_col, _ = where(0)
    work[0 : 2 * UNIT, :] = jnp.zeros((2 * UNIT, UNIT), BF16)
    for at in range(0, UNIT, chunk):
        small[at : at + chunk, :] = distances(first_row, first_col, at)
    lax.fori_loop(0, units, step, 0)
    last_row, last_col, both = where(units - 1)
    for at in range(0, UNIT, chunk):
        products(((units - 1) % 2) * UNIT, last_row, last_col, both, at)
    for row in range(3):
        rows_out[row] = acc_r[:, row * size : (row + 1) * size]
    for hop in range(HOPS + 1):
        cols_out[hop] = acc_c[:, hop * size : (hop + 1) * size]


def vmem(count):
    return [pl.BlockSpec(memory_space=VMEM)] * count


def local(points, scales, vectors, plan):
    size = points.shape[1]
    own = jnp.concatenate([points, vectors], 0)
    stack = own.shape[0]
    smem = [pl.BlockSpec(memory_space=pltpu.SMEM)]
    shard = jax.ShapeDtypeStruct((stack, size), F32)
    dma = pltpu.SemaphoreType.DMA
    cols, far, near = pl.pallas_call(
        fetch_kernel,
        out_shape=(jax.ShapeDtypeStruct((HOPS, stack, size), F32), shard, shard),
        in_specs=smem + vmem(1),
        out_specs=vmem(3),
        scratch_shapes=[VMEM((3, stack, size), F32), VMEM((4, stack, size), F32), dma((9,)), dma((9,))],
        compiler_params=pltpu.CompilerParams(collective_id=0, has_side_effects=True),
    )(plan, own)
    row_sums, col_sums = pl.pallas_call(
        pair_kernel,
        out_shape=(
            jax.ShapeDtypeStruct((3, RHS, size), F32),
            jax.ShapeDtypeStruct((HOPS + 1, RHS, size), F32),
        ),
        in_specs=vmem(5),
        out_specs=vmem(2),
        scratch_shapes=[
            VMEM((UNIT, UNIT), F32),
            VMEM((2 * UNIT + 3 * size, UNIT), BF16),
            VMEM((DEPTH, (HOPS + 1) * size), BF16),
            VMEM((RHS, (HOPS + 1) * size), BF16),
            VMEM((RHS, 3 * size), BF16),
            VMEM((RHS, 3 * size), F32),
            VMEM((RHS, (HOPS + 1) * size), F32),
        ],
        compiler_params=pltpu.CompilerParams(vmem_limit_bytes=40 << 20),
    )(scales[:, None], own, cols, far, near)
    return pl.pallas_call(
        give_kernel,
        out_shape=jax.ShapeDtypeStruct((RHS, size), F32),
        in_specs=smem + vmem(3),
        out_specs=vmem(1)[0],
        scratch_shapes=[
            VMEM((HOPS, RHS, size), F32),
            VMEM((RHS, size), F32),
            VMEM((3, RHS, size), F32),
            VMEM((4, RHS, size), F32),
            dma((9,)),
            dma((9,)),
        ],
        compiler_params=pltpu.CompilerParams(collective_id=1, has_side_effects=True),
    )(plan, vectors, row_sums, col_sums)


def solution(mesh):
    placed = (P(None, ("team", "tile")), P(), P(None, ("team", "tile")), P())
    return jax.shard_map(
        local, mesh=mesh, in_specs=placed, out_specs=P(None, ("team", "tile")), check_vma=False
    )
```

profile of v0, /device:TPU:1, one launch (start us, length us, event | category | flops | bytes accessed | tf_op | source)
XLA Modules:
  0.0 82.6 jit_solution(12548850876848368140)
XLA Ops:
  0.0 0.0 copy-start.7
  0.0 0.8 copy.5.scales_ref
  0.8 0.8 constant_dynamic-update-slice_fusion.1
  1.5 0.0 copy-done.7
  1.5 0.0 copy-start
  1.5 0.6 copy-done
  2.2 23.6 %shard_map.46 = (f32[4,24,1024]{2,1,0:T(8,128)}, f32[24,1024]{1,0:T(8,128)}, f32[24,1024]{1,0:T(8,128)}) custom-call(s32[2]{0:T(128)} %plan_ref.3, f32[24,1024]{1,0:T(8,128)} %copy-done), custom_call_target="tpu_custom_call" | custom-call | tf_op jit(solution)/shard_map/pallas_call | solution.py:245
  25.8 0.0 copy-start.1
  25.8 0.9 %copy-done.1 = f32[24,1024]{1,0:T(8,128)S(1)} copy-done((f32[24,1024]{1,0:T(8,128)S(1)}, f32[24,1024]{1,0:T(8,128)}, u32[]{:S(2)}) %copy-start.1) | copy-done | bytes 98328
  26.7 0.0 copy-start.2
  26.7 1.0 %copy-done.2 = f32[4,24,1024]{2,1,0:T(8,128)S(1)} copy-done((f32[4,24,1024]{2,1,0:T(8,128)S(1)}, f32[4,24,1024]{2,1,0:T(8,128)}, u32[]{:S(2)}) %copy-start.2) | copy-done | bytes 393240
  27.7 0.0 copy-start.5
  27.7 0.9 %copy-done.5 = f32[24,1024]{1,0:T(8,128)S(1)} copy-done((f32[24,1024]{1,0:T(8,128)S(1)}, f32[24,1024]{1,0:T(8,128)}, u32[]{:S(2)}) %copy-start.5) | copy-done | bytes 98328
  28.5 0.0 copy-start.6
  28.6 0.9 %copy-done.6 = f32[24,1024]{1,0:T(8,128)S(1)} copy-done((f32[24,1024]{1,0:T(8,128)S(1)}, f32[24,1024]{1,0:T(8,128)}, u32[]{:S(2)}) %copy-start.6) | copy-done | bytes 98328
  29.4 31.5 %shard_map.47 = (f32[3,16,1024]{2,1,0:T(8,128)S(1)}, f32[5,16,1024]{2,1,0:T(8,128)S(1)}) custom-call(f32[8,1]{1,0:T(8,128)S(1)} %copy.5.scales_ref, f32[24,1024]{1,0:T(8,128)S(1)} %copy-done.1, f32[4,24,1024]{2,1,0:T(8,128)S(1)} %copy-done.2, f32[24,1024]{1,0:T(8,128)S(1)} %copy-done.5, f32[24,1024]{1,0:T(8,128)S(1)} %copy-done.6), custom_call_target="tpu_custom_call" | custom-call | tf_op jit(solution)/shard_map/pallas_call | solution.py:253
  60.9 0.0 copy-start.3
  60.9 0.7 copy-done.3
  61.6 0.0 copy-start.4
  61.6 0.7 copy-done.4
  62.3 18.8 %shard_map.48 = f32[16,1024]{1,0:T(8,128)} custom-call(s32[2]{0:T(128)} %plan_ref.3, f32[16,1024]{1,0:T(8,128)} %vec_ref.1, f32[3,16,1024]{2,1,0:T(8,128)} %copy-done.4, f32[5,16,1024]{2,1,0:T(8,128)} %copy-done.3), custom_call_target="tpu_custom_call" | custom-call | tf_op jit(solution)/shard_map/pallas_call | solution.py:272
  81.1 1.5 %copy.8 = f32[16,1024]{1,0:T(8,128)} copy(f32[16,1024]{1,0:T(8,128)} %shard_map.48) | data formatting | bytes 131072
  (1 shorter events, 0.0 us)
Async XLA Ops:
  0.0 1.5 %copy-start.7 = (f32[16,1024]{1,0:T(8,128)S(1)}, f32[16,1024]{1,0:T(8,128)}, u32[]{:S(2)}) copy-start(f32[16,1024]{1,0:T(8,128)} %vec_ref.1) | copy-start | bytes 196612
  1.5 0.6 copy-start
  25.8 0.9 %copy-start.1 = (f32[24,1024]{1,0:T(8,128)S(1)}, f32[24,1024]{1,0:T(8,128)}, u32[]{:S(2)}) copy-start(f32[24,1024]{1,0:T(8,128)} %copy-done) | copy-start | bytes 294916
  26.7 1.0 %copy-start.2 = (f32[4,24,1024]{2,1,0:T(8,128)S(1)}, f32[4,24,1024]{2,1,0:T(8,128)}, u32[]{:S(2)}) copy-start(f32[4,24,1024]{2,1,0:T(8,128)} %get-tuple-element.10.cols_ref) | copy-start | bytes 1179652
  27.7 0.9 %copy-start.5 = (f32[24,1024]{1,0:T(8,128)S(1)}, f32[24,1024]{1,0:T(8,128)}, u32[]{:S(2)}) copy-start(f32[24,1024]{1,0:T(8,128)} %get-tuple-element.11.far_ref) | copy-start | bytes 294916
  28.5 0.9 %copy-start.6 = (f32[24,1024]{1,0:T(8,128)S(1)}, f32[24,1024]{1,0:T(8,128)}, u32[]{:S(2)}) copy-start(f32[24,1024]{1,0:T(8,128)} %get-tuple-element.12.near_ref) | copy-start | bytes 294916
  60.9 0.7 copy-start.3
  61.6 0.7 copy-start.4
where the time goes:
time: 84 us; the launch traced here: 82.6 us
  Pallas kernels  73.8 us (88%)
  local copies, waits for them, and re-layouts  8.69 us (10%)
    pallas_call x1, Pallas kernels, local(): pl.pallas_call(pair_kernel, out_shape=(jax.ShapeDtypeStruct((3, RHS, size...  31.5 us
    pallas_call x1, Pallas kernels, local(): pl.pallas_call(fetch_kernel, out_shape=(jax.ShapeDtypeStruct((HOPS, stack...  23.6 us
    pallas_call x1, Pallas kernels, local(): pl.pallas_call(give_kernel, out_shape=jax.ShapeDtypeStruct((RHS, size), F...  18.8 us
    unnamed x18, local copies, waits for them, and re-layouts  7.92 us

commit v1 on v0

v1 whole, which is shorter than its diff:
```python
import functools
import math

import jax
import jax.numpy as jnp
from jax import lax
from jax.experimental import pallas as pl
from jax.experimental.pallas import tpu as pltpu
from jax.sharding import PartitionSpec as P

MESH = pl.DeviceIdType.MESH
VMEM = pltpu.VMEM
F32 = jnp.float32
BF16 = jnp.bfloat16

SHRINK = math.sqrt(0.05)
RATE = -10.0 / math.log(2.0)
COORDS = 8
RHS = 16
DEPTH = 64
UNIT = 512
HOPS = 4
PER_ROW = 17


def tile_id(offset):
    count = lax.axis_size("tile")
    return {"tile": lax.rem(lax.axis_index("tile") + offset + count, count)}


def team_id(pairing):
    me = lax.axis_index("team")
    bits = lax.axis_size("team").bit_length() - 1
    other = me * 0
    for bit in range(bits):
        mine = lax.rem(me // (1 << bit), 2)
        other = other + (1 << bit) * (1 - mine if pairing >> bit & 1 else mine)
    return {"team": other}


def greet(friends):
    barrier = pltpu.get_barrier_semaphore()
    for friend in friends:
        pl.semaphore_signal(barrier, inc=1, device_id=friend, device_id_type=MESH)
    pl.semaphore_wait(barrier, len(friends))


def remote(src, dst, send, recv, target):
    return pltpu.make_async_remote_copy(
        src_ref=src, dst_ref=dst, send_sem=send, recv_sem=recv, device_id=target, device_id_type=MESH
    )


def pieces(value, count):
    out = []
    for _ in range(count):
        piece = value.astype(BF16).astype(F32)
        out.append(piece)
        value = value - piece
    return out


def split(shard, scales):
    scaled = shard[:COORDS] / scales * SHRINK
    one, two, three = pieces(scaled, 3)
    norm = jnp.sum(scaled * scaled, axis=0, keepdims=True)
    return one, two, three, pieces(norm, 3)


def place(parts, size):
    row = lax.broadcasted_iota(jnp.int32, (8, size), 0)
    out = jnp.zeros((8, size), F32)
    for at, part in enumerate(parts):
        out = jnp.where(row == at, part, out)
    return out


def col_operand(shard, scales):
    one, two, three, norms = split(shard, scales)
    unit = jnp.ones_like(norms[0])
    tail = place(norms + [unit] * 3, shard.shape[1])
    return jnp.concatenate([one, one, one, two, two, three, tail, jnp.zeros_like(tail)], 0).astype(BF16)


def row_operand(shard, scales):
    one, two, three, norms = split(shard, scales)
    unit = jnp.ones_like(norms[0])
    tail = place([unit] * 3 + norms, shard.shape[1])
    stack = [-2.0 * one, -2.0 * two, -2.0 * three, -2.0 * one, -2.0 * two, -2.0 * one, tail]
    stack += [jnp.zeros_like(tail)] * 9
    return jnp.concatenate(stack, 0).T


def matern(small):
    small = jnp.maximum(small, 1e-30)
    w = small * lax.rsqrt(small)
    return ((w * (w + 0.3) + 0.03) * jnp.exp2(w * RATE)).astype(BF16)


def kernel(
    pairing,
    scales_ref,
    points_ref,
    vectors_ref,
    out_ref,
    own,
    came,
    small,
    work,
    col_x,
    col_v,
    row_v,
    acc_r,
    acc_c,
    back,
    sends,
    recvs,
):
    size = points_ref.shape[1]
    halves = size // UNIT
    units = 3 * PER_ROW
    far_team, near_team = team_id(15), team_id(pairing)
    own[0:COORDS, :] = points_ref[...]
    own[COORDS : COORDS + RHS, :] = vectors_ref[...]
    greet([tile_id(step) for step in range(1, lax.axis_size("tile"))] + [far_team, near_team])

    def fetch(slot):
        target = tile_id(-1 - slot) if slot < HOPS else (far_team if slot == HOPS else near_team)
        return remote(own, came.at[slot], sends.at[slot], recvs.at[slot], target)

    def give(slot):
        target = tile_id(1 + slot) if slot < HOPS else (far_team if slot == HOPS else near_team)
        if slot < HOPS:
            src = acc_c.at[:, (slot + 1) * size : (slot + 2) * size]
        else:
            src = acc_r.at[:, (slot - 3) * size : (slot - 2) * size]
        return remote(src, back.at[slot], sends.at[6 + slot], recvs.at[6 + slot], target)

    for slot in (0, 4, 1, 2, 3, 5):
        fetch(slot).start()

    line = lax.broadcasted_iota(jnp.int32, (COORDS, 1), 0)
    scales = jnp.zeros((COORDS, 1), F32)
    for coord in range(COORDS):
        scales = jnp.where(line == coord, scales_ref[coord], scales)

    def ready_row(shard, row):
        work[2 * UNIT + row * size : 2 * UNIT + (row + 1) * size, 0:128] = row_operand(shard, scales).astype(BF16)
        row_v[:, row * size : (row + 1) * size] = shard[COORDS:].astype(BF16)

    def ready_col(shard, hop):
        col_x[:, hop * size : (hop + 1) * size] = col_operand(shard, scales)
        col_v[:, hop * size : (hop + 1) * size] = shard[COORDS:].astype(BF16)

    ready_row(own[...], 0)
    ready_col(own[...], 0)
    acc_r[...] = jnp.zeros_like(acc_r)
    acc_c[...] = jnp.zeros_like(acc_c)
    upper = (lax.axis_index("tile") >= lax.axis_size("tile") // 2).astype(jnp.int32)

    def where(unit):
        shard = jnp.where(unit < 7, 0, jnp.where(unit < 24, 1, jnp.where(unit < 41, 2, 0)))
        item = jnp.where(unit < 7, unit, jnp.where(unit < 24, unit - 7, unit - 24))
        item = jnp.where(unit < 41, item, jnp.where(unit < 43, unit - 26, jnp.where(unit < 47, unit - 32, unit - 40)))
        inner = item - 3
        row = jnp.where(item < 3, (item == 1).astype(jnp.int32), lax.rem(inner // 2, 2))
        row = jnp.where(item == 15, upper, jnp.where(item == 16, 1, row))
        col = jnp.where(item < 3, (item > 0).astype(jnp.int32), 2 * (1 + inner // 4) + lax.rem(inner, 2))
        col = jnp.where(item == 15, 8, jnp.where(item == 16, 8 + upper, col))
        one_way = (item < 2).astype(F32)
        return pl.multiple_of((shard * halves + row) * UNIT, UNIT), pl.multiple_of(col * UNIT, UNIT), 1.0 - one_way

    chunk = 256

    def distances(row, col, at):
        rows = work[pl.ds(pl.multiple_of(2 * UNIT + row + at, chunk), chunk), 0:DEPTH]
        return jnp.dot(rows, col_x[:, pl.ds(col, UNIT)], preferred_element_type=F32)

    def products(base, row, col, both, at):
        part = work[pl.ds(pl.multiple_of(base + at, chunk), chunk), :]
        rows = pl.ds(pl.multiple_of(row + at, chunk), chunk)
        cols = pl.ds(col, UNIT)
        acc_c[:, cols] += jnp.dot(row_v[:, rows], part, preferred_element_type=F32)
        acc_r[:, rows] += both * lax.dot_general(
            col_v[:, cols], part, (((1,), (1,)), ((), ())), preferred_element_type=F32
        )

    def step(unit, carry):
        for start, slot in ((3, 0), (7, 4), (14, 1), (18, 2), (22, 3), (24, 5)):

            @pl.when(unit == start - 1)
            def _(slot=slot):
                fetch(slot).wait_recv()
                if slot < HOPS:
                    ready_col(came[slot], slot + 1)
                else:
                    ready_row(came[slot], slot - 3)

        for after, slots in ((25, (4,)), (42, (5, 0)), (44, (3,)), (48, (2,))):

            @pl.when(unit == after)
            def _(slots=slots):
                for slot in slots:
                    give(slot).start()

        base = pl.multiple_of(lax.rem(unit, 2) * UNIT, UNIT)
        last = pl.multiple_of(UNIT - base, UNIT)
        next_row, next_col, _ = where(jnp.minimum(unit + 1, units - 1))
        last_row, last_col, both = where(jnp.maximum(unit - 1, 0))
        for at in range(0, UNIT, chunk):
            fresh = distances(next_row, next_col, at)
            products(last, last_row, last_col, both, at)
            for line in range(at, at + chunk, 16):
                work[pl.ds(pl.multiple_of(base + line, 16), 16), :] = matern(small[line : line + 16, :])
            small[at : at + chunk, :] = fresh
        return carry

    first_row, first_col, _ = where(0)
    work[0 : 2 * UNIT, :] = jnp.zeros((2 * UNIT, UNIT), BF16)
    for at in range(0, UNIT, chunk):
        small[at : at + chunk, :] = distances(first_row, first_col, at)
    lax.fori_loop(0, units, step, 0)
    last_row, last_col, both = where(units - 1)
    for at in range(0, UNIT, chunk):
        products(((units - 1) % 2) * UNIT, last_row, last_col, both, at)
    give(1).start()
    total = 0.5 * vectors_ref[...] + acc_r[:, 0:size] + acc_c[:, 0:size]
    for slot in (4, 5, 0, 3, 2, 1):
        give(slot).wait_recv()
        total = total + back[slot]
    out_ref[...] = total
    for slot in range(6):
        fetch(slot).wait_send()
        give(slot).wait_send()


def vmem(count):
    return [pl.BlockSpec(memory_space=VMEM)] * count


def paired(pairing):
    def call(scales, points, vectors):
        size = points.shape[1]
        dma = pltpu.SemaphoreType.DMA
        return pl.pallas_call(
            functools.partial(kernel, pairing),
            out_shape=jax.ShapeDtypeStruct((RHS, size), F32),
            in_specs=[pl.BlockSpec(memory_space=pltpu.SMEM)] + vmem(2),
            out_specs=vmem(1)[0],
            scratch_shapes=[
                VMEM((COORDS + RHS, size), F32),
                VMEM((6, COORDS + RHS, size), F32),
                VMEM((UNIT, UNIT), F32),
                VMEM((2 * UNIT + 3 * size, UNIT), BF16),
                VMEM((DEPTH, (HOPS + 1) * size), BF16),
                VMEM((RHS, (HOPS + 1) * size), BF16),
                VMEM((RHS, 3 * size), BF16),
                VMEM((RHS, 3 * size), F32),
                VMEM((RHS, (HOPS + 1) * size), F32),
                VMEM((6, RHS, size), F32),
                dma((12,)),
                dma((12,)),
            ],
            compiler_params=pltpu.CompilerParams(
                collective_id=pairing - 1, has_side_effects=True, vmem_limit_bytes=40 << 20
            ),
        )(scales, points, vectors)

    return call


def local(points, scales, vectors, plan):
    pairing = plan[0] + plan[1] - 15
    return lax.switch(pairing - 1, [paired(number) for number in range(1, 15)], scales, points, vectors)


def solution(mesh):
    placed = (P(None, ("team", "tile")), P(), P(None, ("team", "tile")), P())
    return jax.shard_map(
        local, mesh=mesh, in_specs=placed, out_specs=P(None, ("team", "tile")), check_vma=False
    )
```

time: 84 us -> 53.7 us (0.64); the launches traced: 82.6 us -> 53.5 us
  Pallas kernels: 73.8 us -> 49.6 us
  local copies, waits for them, and re-layouts: 8.69 us -> 2.52 us
  between operations: 0.05 us -> 1.22 us
    pallas_call x3 -> x1, Pallas kernels: 73.8 us -> 49.6 us  [call(): pl.pallas_call(functools.partial(kernel, pairing), out_shape=jax.ShapeDty...]
    unnamed x18 -> x5, local copies, waits for them, and re-layouts: 7.92 us -> 1.94 us
where the time goes in v1:
time: 53.7 us; the launch traced here: 53.5 us
  Pallas kernels  49.6 us (92%)
  local copies, waits for them, and re-layouts  2.52 us (5%)
  between operations  1.22 us (2%)
    pallas_call x1, Pallas kernels, call(): pl.pallas_call(functools.partial(kernel, pairing), out_shape=jax.ShapeDty...  49.6 us
    unnamed x5, local copies, waits for them, and re-layouts  1.94 us

profile of v1, /device:TPU:1, one launch (start us, length us, event | category | flops | bytes accessed | tf_op | source)
XLA Modules:
  0.0 53.5 jit_solution(5830769917082938559)
XLA Ops:
  0.0 0.0 copy-start.1
  0.0 0.7 %copy-done.1 = s32[2]{0:T(128)S(1)} copy-done((s32[2]{0:T(128)S(1)}, s32[2]{0:T(128)}, u32[]{:S(2)}) %copy-start.1) | copy-done | bytes 32
  0.7 0.6 %fusion = (s32[1]{0:T(128)}, s32[1]{0:T(128)}) fusion(s32[2]{0:T(128)S(1)} %copy-done.1), kind=kLoop, calls=%fused_computation | loop fusion | bytes 16 | tf_op jit(solution)/shard_map/slice | solution.py:273
  2.4 0.0 copy-start
  2.5 0.6 %copy-done = f32[8]{0:T(128)S(1)} copy-done((f32[8]{0:T(128)S(1)}, f32[8]{0:T(128)}, u32[]{:S(2)}) %copy-start) | copy-done | bytes 56
  3.1 49.8 %conditional.1 = (f32[16,1024]{1,0:T(8,128)S(1)}) conditional(s32[]{:T(128)} %bitcast, (f32[8]{0:T(128)S(1)}, f32[8,1024]{1,0:T(8,128)}, f32[16,1024]{1,0:T(8,128)}) %tuple.77, (f32[8]{0:T(128)S(1)}, f32[8,1024]{1,0:T(8,128)}, f32[16,1024]{1,0:T(8,128)}) %tuple.78, (f32[8]{0:T(128)S(1)}, f32[8,1024]{1,0:T(8,128)}, ...), branch_computations={%region_0.0_spmd, %region_1.0_spmd, %region_2.0_spmd, %region_3.0_... | conditional | bytes 8 | solution.py:274
  3.1 49.6 %branch_4_fun.1 = f32[16,1024]{1,0:T(8,128)S(1)} custom-call(f32[8]{0:T(128)S(1)} %get-tuple-element.116.scales_ref, f32[8,1024]{1,0:T(8,128)} %get-tuple-element.117.points_ref, f32[16,1024]{1,0:T(8,128)} %get-tuple-element.118.vectors_ref), custom_call_target="tpu_custom_call" | custom-call | tf_op jit(solution)/shard_map/cond/branch_4_fun/pallas_call | solution.py:245
  52.9 0.6 %copy.34 = f32[16,1024]{1,0:T(8,128)} copy(f32[16,1024]{1,0:T(8,128)S(1)} %get-tuple-element.146) | data formatting | bytes 131072
Async XLA Ops:
  0.0 0.7 %copy-start.1 = (s32[2]{0:T(128)S(1)}, s32[2]{0:T(128)}, u32[]{:S(2)}) copy-start(s32[2]{0:T(128)} %param.21) | copy-start | bytes 28
  2.4 0.7 %copy-start = (f32[8]{0:T(128)S(1)}, f32[8]{0:T(128)}, u32[]{:S(2)}) copy-start(f32[8]{0:T(128)} %param.19) | copy-start | bytes 100

commit v2 on v1

--- a/solution.py
+++ b/solution.py
@@ -19,8 +19,10 @@
 RHS = 16
 DEPTH = 64
 UNIT = 512
+CHUNK = 256
 HOPS = 4
-PER_ROW = 17
+HOME = 17
+AWAY = 16
 
 
 def tile_id(offset):
@@ -106,7 +108,8 @@
     own,
     came,
     small,
-    work,
+    held,
+    row_x,
     col_x,
     col_v,
     row_v,
@@ -118,8 +121,9 @@
 ):
     size = points_ref.shape[1]
     halves = size // UNIT
-    units = 3 * PER_ROW
+    units = HOME + 2 * AWAY
     far_team, near_team = team_id(15), team_id(pairing)
+    me = lax.axis_index("team")
     own[0:COORDS, :] = points_ref[...]
     own[COORDS : COORDS + RHS, :] = vectors_ref[...]
     greet([tile_id(step) for step in range(1, lax.axis_size("tile"))] + [far_team, near_team])
@@ -145,7 +149,7 @@
         scales = jnp.where(line == coord, scales_ref[coord], scales)
 
     def ready_row(shard, row):
-        work[2 * UNIT + row * size : 2 * UNIT + (row + 1) * size, 0:128] = row_operand(shard, scales).astype(BF16)
+        row_x[row * size : (row + 1) * size, :] = row_operand(shard, scales).astype(BF16)
         row_v[:, row * size : (row + 1) * size] = shard[COORDS:].astype(BF16)
 
     def ready_col(shard, hop):
@@ -157,36 +161,40 @@
     acc_r[...] = jnp.zeros_like(acc_r)
     acc_c[...] = jnp.zeros_like(acc_c)
     upper = (lax.axis_index("tile") >= lax.axis_size("tile") // 2).astype(jnp.int32)
+    far_shift = (me > far_team["team"]).astype(jnp.int32)
+    near_shift = (me > near_team["team"]).astype(jnp.int32)
 
     def where(unit):
-        shard = jnp.where(unit < 7, 0, jnp.where(unit < 24, 1, jnp.where(unit < 41, 2, 0)))
-        item = jnp.where(unit < 7, unit, jnp.where(unit < 24, unit - 7, unit - 24))
-        item = jnp.where(unit < 41, item, jnp.where(unit < 43, unit - 26, jnp.where(unit < 47, unit - 32, unit - 40)))
-        inner = item - 3
-        row = jnp.where(item < 3, (item == 1).astype(jnp.int32), lax.rem(inner // 2, 2))
-        row = jnp.where(item == 15, upper, jnp.where(item == 16, 1, row))
-        col = jnp.where(item < 3, (item > 0).astype(jnp.int32), 2 * (1 + inner // 4) + lax.rem(inner, 2))
-        col = jnp.where(item == 15, 8, jnp.where(item == 16, 8 + upper, col))
-        one_way = (item < 2).astype(F32)
-        return pl.multiple_of((shard * halves + row) * UNIT, UNIT), pl.multiple_of(col * UNIT, UNIT), 1.0 - one_way
-
-    chunk = 256
+        far, near = unit >= 7, unit >= 7 + AWAY
+        late = unit >= 7 + 2 * AWAY
+        shard = jnp.where(late, 0, near.astype(jnp.int32) + far.astype(jnp.int32))
+        index = jnp.where(far, jnp.where(near, unit - 7 - AWAY, unit - 7), unit - 3)
+        place = jnp.where(far, jnp.where(near, near_shift, far_shift), 1)
+        index = jnp.where(late, jnp.where(unit < 45, unit - 41, unit - 45), index)
+        place = jnp.where(late, jnp.where(unit < 45, 3, 2), place)
+        row = lax.rem(index // 2, 2)
+        col = 2 * (place + index // 4) + lax.rem(index, 2)
+        row = jnp.where(unit < 3, (unit == 1).astype(jnp.int32), row)
+        col = jnp.where(unit < 3, (unit > 0).astype(jnp.int32), col)
+        row = jnp.where(unit == 39, upper, jnp.where(unit == 40, 1, row))
+        col = jnp.where(unit == 39, 8, jnp.where(unit == 40, 8 + upper, col))
+        return (shard * halves + row) * UNIT, col * UNIT, (unit >= 2).astype(F32)
 
     def distances(row, col, at):
-        rows = work[pl.ds(pl.multiple_of(2 * UNIT + row + at, chunk), chunk), 0:DEPTH]
-        return jnp.dot(rows, col_x[:, pl.ds(col, UNIT)], preferred_element_type=F32)
-
-    def products(base, row, col, both, at):
-        part = work[pl.ds(pl.multiple_of(base + at, chunk), chunk), :]
-        rows = pl.ds(pl.multiple_of(row + at, chunk), chunk)
-        cols = pl.ds(col, UNIT)
+        rows = row_x[pl.ds(pl.multiple_of(row + at, CHUNK), CHUNK), 0:DEPTH]
+        return jnp.dot(rows, col_x[:, pl.ds(pl.multiple_of(col, UNIT), UNIT)], preferred_element_type=F32)
+
+    def products(row, col, both, at):
+        part = held[at // CHUNK]
+        rows = pl.ds(pl.multiple_of(row + at, CHUNK), CHUNK)
+        cols = pl.ds(pl.multiple_of(col, UNIT), UNIT)
         acc_c[:, cols] += jnp.dot(row_v[:, rows], part, preferred_element_type=F32)
         acc_r[:, rows] += both * lax.dot_general(
             col_v[:, cols], part, (((1,), (1,)), ((), ())), preferred_element_type=F32
         )
 
     def step(unit, carry):
-        for start, slot in ((3, 0), (7, 4), (14, 1), (18, 2), (22, 3), (24, 5)):
+        for start, slot in ((3, 0), (7, 4), (11, 1), (15, 2), (19, 3), (23, 5)):
 
             @pl.when(unit == start - 1)
             def _(slot=slot):
@@ -196,33 +204,32 @@
                 else:
                     ready_row(came[slot], slot - 3)
 
-        for after, slots in ((25, (4,)), (42, (5, 0)), (44, (3,)), (48, (2,))):
+        for after, slots in ((24, (4,)), (32, (0,)), (40, (5,)), (42, (3,)), (46, (2,))):
 
             @pl.when(unit == after)
             def _(slots=slots):
                 for slot in slots:
                     give(slot).start()
 
-        base = pl.multiple_of(lax.rem(unit, 2) * UNIT, UNIT)
-        last = pl.multiple_of(UNIT - base, UNIT)
-        next_row, next_col, _ = where(jnp.minimum(unit + 1, units - 1))
-        last_row, last_col, both = where(jnp.maximum(unit - 1, 0))
-        for at in range(0, UNIT, chunk):
-            fresh = distances(next_row, next_col, at)
-            products(last, last_row, last_col, both, at)
-            for line in range(at, at + chunk, 16):
-                work[pl.ds(pl.multiple_of(base + line, 16), 16), :] = matern(small[line : line + 16, :])
-            small[at : at + chunk, :] = fresh
-        return carry
-
-    first_row, first_col, _ = where(0)
-    work[0 : 2 * UNIT, :] = jnp.zeros((2 * UNIT, UNIT), BF16)
-    for at in range(0, UNIT, chunk):
-        small[at : at + chunk, :] = distances(first_row, first_col, at)
-    lax.fori_loop(0, units, step, 0)
-    last_row, last_col, both = where(units - 1)
-    for at in range(0, UNIT, chunk):
-        products(((units - 1) % 2) * UNIT, last_row, last_col, both, at)
+        last, current = carry
+        following = where(jnp.minimum(unit + 1, units - 1))
+        for at in range(0, UNIT, CHUNK):
+            fresh = distances(following[0], following[1], at)
+            if at == 0:
+                products(*last, UNIT - CHUNK)
+            else:
+                products(*current, at - CHUNK)
+            for line in range(0, CHUNK, 16):
+                held[at // CHUNK, line : line + 16, :] = matern(small[at + line : at + line + 16, :])
+            small[at : at + CHUNK, :] = fresh
+        return current, following
+
+    first = where(jnp.int32(0))
+    held[...] = jnp.zeros_like(held)
+    for at in range(0, UNIT, CHUNK):
+        small[at : at + CHUNK, :] = distances(first[0], first[1], at)
+    last, _ = lax.fori_loop(0, units, step, (first, first))
+    products(*last, UNIT - CHUNK)
     give(1).start()
     total = 0.5 * vectors_ref[...] + acc_r[:, 0:size] + acc_c[:, 0:size]
     for slot in (4, 5, 0, 3, 2, 1):
@@ -251,7 +258,8 @@
                 VMEM((COORDS + RHS, size), F32),
                 VMEM((6, COORDS + RHS, size), F32),
                 VMEM((UNIT, UNIT), F32),
-                VMEM((2 * UNIT + 3 * size, UNIT), BF16),
+                VMEM((UNIT // CHUNK, CHUNK, UNIT), BF16),
+                VMEM((3 * size, 128), BF16),
                 VMEM((DEPTH, (HOPS + 1) * size), BF16),
                 VMEM((RHS, (HOPS + 1) * size), BF16),
                 VMEM((RHS, 3 * size), BF16),

time: 53.7 us -> 49.7 us (0.926)
  Pallas kernels: 49.6 us -> 45.5 us
    pallas_call x1, Pallas kernels: 49.6 us -> 45.5 us  [call(): pl.pallas_call(functools.partial(kernel, pairing), out_shape=jax.ShapeDty...]
where the time goes in v2:
time: 49.7 us; the launch traced here: 49.5 us
  Pallas kernels  45.5 us (92%)
  local copies, waits for them, and re-layouts  2.52 us (5%)
  between operations  1.22 us (2%)
    pallas_call x1, Pallas kernels, call(): pl.pallas_call(functools.partial(kernel, pairing), out_shape=jax.ShapeDty...  45.5 us
    unnamed x5, local copies, waits for them, and re-layouts  1.94 us

profile of v2, /device:TPU:1, one launch (start us, length us, event | category | flops | bytes accessed | tf_op | source)
XLA Modules:
  0.0 49.5 jit_solution(9041075547523187884)
XLA Ops:
  0.0 0.0 copy-start.1
  0.0 0.7 %copy-done.1 = s32[2]{0:T(128)S(1)} copy-done((s32[2]{0:T(128)S(1)}, s32[2]{0:T(128)}, u32[]{:S(2)}) %copy-start.1) | copy-done | bytes 32
  0.7 0.6 %fusion = (s32[1]{0:T(128)}, s32[1]{0:T(128)}) fusion(s32[2]{0:T(128)S(1)} %copy-done.1), kind=kLoop, calls=%fused_computation | loop fusion | bytes 16 | tf_op jit(solution)/shard_map/slice | solution.py:281
  2.4 0.0 copy-start
  2.5 0.6 %copy-done = f32[8]{0:T(128)S(1)} copy-done((f32[8]{0:T(128)S(1)}, f32[8]{0:T(128)}, u32[]{:S(2)}) %copy-start) | copy-done | bytes 56
  3.1 45.7 %conditional.1 = (f32[16,1024]{1,0:T(8,128)S(1)}) conditional(s32[]{:T(128)} %bitcast, (f32[8]{0:T(128)S(1)}, f32[8,1024]{1,0:T(8,128)}, f32[16,1024]{1,0:T(8,128)}) %tuple.77, (f32[8]{0:T(128)S(1)}, f32[8,1024]{1,0:T(8,128)}, f32[16,1024]{1,0:T(8,128)}) %tuple.78, (f32[8]{0:T(128)S(1)}, f32[8,1024]{1,0:T(8,128)}, ...), branch_computations={%region_0.0_spmd, %region_1.0_spmd, %region_2.0_spmd, %region_3.0_... | conditional | bytes 8 | solution.py:282
  3.1 45.5 %branch_0_fun.1 = f32[16,1024]{1,0:T(8,128)S(1)} custom-call(f32[8]{0:T(128)S(1)} %get-tuple-element.90.scales_ref, f32[8,1024]{1,0:T(8,128)} %get-tuple-element.91.points_ref, f32[16,1024]{1,0:T(8,128)} %get-tuple-element.96.vectors_ref), custom_call_target="tpu_custom_call" | custom-call | tf_op jit(solution)/shard_map/cond/branch_0_fun/pallas_call | solution.py:252
  48.8 0.6 %copy.34 = f32[16,1024]{1,0:T(8,128)} copy(f32[16,1024]{1,0:T(8,128)S(1)} %get-tuple-element.146) | data formatting | bytes 131072
Async XLA Ops:
  0.0 0.7 %copy-start.1 = (s32[2]{0:T(128)S(1)}, s32[2]{0:T(128)}, u32[]{:S(2)}) copy-start(s32[2]{0:T(128)} %param.21) | copy-start | bytes 28
  2.4 0.7 %copy-start = (f32[8]{0:T(128)S(1)}, f32[8]{0:T(128)}, u32[]{:S(2)}) copy-start(f32[8]{0:T(128)} %param.19) | copy-start | bytes 100

commit v3 on v2

--- a/solution.py
+++ b/solution.py
@@ -21,8 +21,8 @@
 UNIT = 512
 CHUNK = 256
 HOPS = 4
-HOME = 17
-AWAY = 16
+ORDER = ((0, 0), (0, 1), (2, 0), (2, 1), (2, 2), (2, 3), (0, 3), (0, 4), (1, 3), (1, 2), (1, 1), (1, 0), (0, 2))
+SENDS = {1: -1, 5: -1, 0: -1, 2: -1, 3: -1, 4: -1}
 
 
 def tile_id(offset):
@@ -121,7 +121,6 @@
 ):
     size = points_ref.shape[1]
     halves = size // UNIT
-    units = HOME + 2 * AWAY
     far_team, near_team = team_id(15), team_id(pairing)
     me = lax.axis_index("team")
     own[0:COORDS, :] = points_ref[...]
@@ -140,8 +139,9 @@
             src = acc_r.at[:, (slot - 3) * size : (slot - 2) * size]
         return remote(src, back.at[slot], sends.at[6 + slot], recvs.at[6 + slot], target)
 
-    for slot in (0, 4, 1, 2, 3, 5):
-        fetch(slot).start()
+    for slot in SENDS:
+        if SENDS[slot] < 0:
+            fetch(slot).start()
 
     line = lax.broadcasted_iota(jnp.int32, (COORDS, 1), 0)
     scales = jnp.zeros((COORDS, 1), F32)
@@ -161,23 +161,32 @@
     acc_r[...] = jnp.zeros_like(acc_r)
     acc_c[...] = jnp.zeros_like(acc_c)
     upper = (lax.axis_index("tile") >= lax.axis_size("tile") // 2).astype(jnp.int32)
-    far_shift = (me > far_team["team"]).astype(jnp.int32)
-    near_shift = (me > near_team["team"]).astype(jnp.int32)
+    shifts = [jnp.int32(0)] + [(me > team["team"]).astype(jnp.int32) for team in (far_team, near_team)]
+    counts = [3 if group == (0, 0) else 2 if group == (0, HOPS) else 4 for group in ORDER]
+    starts = [sum(counts[:number]) for number in range(len(ORDER))]
+    units = sum(counts)
+    first_use, last_use = {}, {}
+    for (shard, place), start, count in zip(ORDER, starts, counts):
+        used = [place - 1] if shard == 0 else [place - 1, place, HOPS - 1 + shard]
+        for slot in used:
+            if slot >= 0:
+                first_use.setdefault(slot, start)
+                last_use[slot] = start + count - 1
 
     def where(unit):
-        far, near = unit >= 7, unit >= 7 + AWAY
-        late = unit >= 7 + 2 * AWAY
-        shard = jnp.where(late, 0, near.astype(jnp.int32) + far.astype(jnp.int32))
-        index = jnp.where(far, jnp.where(near, unit - 7 - AWAY, unit - 7), unit - 3)
-        place = jnp.where(far, jnp.where(near, near_shift, far_shift), 1)
-        index = jnp.where(late, jnp.where(unit < 45, unit - 41, unit - 45), index)
-        place = jnp.where(late, jnp.where(unit < 45, 3, 2), place)
+        shard, place, index = jnp.int32(0), jnp.int32(0), unit
+        for (group_shard, group_place), start in zip(ORDER[1:], starts[1:]):
+            here = unit >= start
+            shard = jnp.where(here, group_shard, shard)
+            place = jnp.where(here, group_place + shifts[group_shard], place)
+            index = jnp.where(here, unit - start, index)
         row = lax.rem(index // 2, 2)
-        col = 2 * (place + index // 4) + lax.rem(index, 2)
+        col = 2 * place + lax.rem(index, 2)
         row = jnp.where(unit < 3, (unit == 1).astype(jnp.int32), row)
         col = jnp.where(unit < 3, (unit > 0).astype(jnp.int32), col)
-        row = jnp.where(unit == 39, upper, jnp.where(unit == 40, 1, row))
-        col = jnp.where(unit == 39, 8, jnp.where(unit == 40, 8 + upper, col))
+        half = starts[ORDER.index((0, HOPS))]
+        row = jnp.where(unit == half, upper, jnp.where(unit == half + 1, 1, row))
+        col = jnp.where(unit == half, 2 * HOPS, jnp.where(unit == half + 1, 2 * HOPS + upper, col))
         return (shard * halves + row) * UNIT, col * UNIT, (unit >= 2).astype(F32)
 
     def distances(row, col, at):
@@ -194,25 +203,26 @@
         )
 
     def step(unit, carry):
-        for start, slot in ((3, 0), (7, 4), (11, 1), (15, 2), (19, 3), (23, 5)):
-
-            @pl.when(unit == start - 1)
-            def _(slot=slot):
-                fetch(slot).wait_recv()
-                if slot < HOPS:
-                    ready_col(came[slot], slot + 1)
-                else:
-                    ready_row(came[slot], slot - 3)
-
-        for after, slots in ((24, (4,)), (32, (0,)), (40, (5,)), (42, (3,)), (46, (2,))):
-
-            @pl.when(unit == after)
-            def _(slots=slots):
-                for slot in slots:
-                    give(slot).start()
-
-        last, current = carry
-        following = where(jnp.minimum(unit + 1, units - 1))
+        for number in range(units):
+            leaving = [slot for slot in SENDS if SENDS[slot] == number]
+            coming = [slot for slot in first_use if first_use[slot] == number + 1]
+            giving = [slot for slot in last_use if last_use[slot] == number - 2]
+            if leaving or coming or giving:
+
+                @pl.when(unit == number)
+                def _(leaving=leaving, coming=coming, giving=giving):
+                    for slot in leaving:
+                        fetch(slot).start()
+                    for slot in giving:
+                        give(slot).start()
+                    for slot in coming:
+                        fetch(slot).wait_recv()
+                        if slot < HOPS:
+                            ready_col(came[slot], slot + 1)
+                        else:
+                            ready_row(came[slot], slot - 3)
+
+        last, current, following = carry
         for at in range(0, UNIT, CHUNK):
             fresh = distances(following[0], following[1], at)
             if at == 0:
@@ -222,17 +232,19 @@
             for line in range(0, CHUNK, 16):
                 held[at // CHUNK, line : line + 16, :] = matern(small[at + line : at + line + 16, :])
             small[at : at + CHUNK, :] = fresh
-        return current, following
+        return current, following, where(jnp.minimum(unit + 2, units - 1))
 
     first = where(jnp.int32(0))
     held[...] = jnp.zeros_like(held)
     for at in range(0, UNIT, CHUNK):
         small[at : at + CHUNK, :] = distances(first[0], first[1], at)
-    last, _ = lax.fori_loop(0, units, step, (first, first))
+    last, _, _ = lax.fori_loop(0, units, step, (first, first, where(jnp.int32(1))))
     products(*last, UNIT - CHUNK)
-    give(1).start()
+    for slot in last_use:
+        if last_use[slot] > units - 3:
+            give(slot).start()
     total = 0.5 * vectors_ref[...] + acc_r[:, 0:size] + acc_c[:, 0:size]
-    for slot in (4, 5, 0, 3, 2, 1):
+    for slot in sorted(last_use, key=lambda slot: last_use[slot]):
         give(slot).wait_recv()
         total = total + back[slot]
     out_ref[...] = total
@@ -270,7 +282,7 @@
                 dma((12,)),
             ],
             compiler_params=pltpu.CompilerParams(
-                collective_id=pairing - 1, has_side_effects=True, vmem_limit_bytes=40 << 20
+                collective_id=pairing - 1, has_side_effects=True, vmem_limit_bytes=60 << 20
             ),
         )(scales, points, vectors)
 
@@ -278,8 +290,8 @@
 
 
 def local(points, scales, vectors, plan):
-    pairing = plan[0] + plan[1] - 15
-    return lax.switch(pairing - 1, [paired(number) for number in range(1, 15)], scales, points, vectors)
+    kernels = [paired(number) for number in range(1, 15)]
+    return lax.switch(jnp.min(plan), [lambda scales, points, vectors: vectors] + kernels, scales, points, vectors)
 
 
 def solution(mesh):

time: 49.7 us -> 47.2 us (0.950)
  Pallas kernels: 45.5 us -> 43.4 us
  other arithmetic: 0 us -> 0.63 us
  local copies, waits for them, and re-layouts: 2.52 us -> 1.96 us
  between operations: 1.22 us -> 0.71 us
    pallas_call x1, Pallas kernels: 45.5 us -> 43.4 us  [call(): pl.pallas_call(functools.partial(kernel, pairing), out_shape=jax.ShapeDty...]
    cond x0 -> x1, local copies, waits for them, and re-layouts: none -> 0.63 us
    reduce_min x0 -> x1, other arithmetic: none -> 0.63 us  [local(): jnp.min(plan)]
    unnamed x5 -> x9, local copies, waits for them, and re-layouts: 1.94 us -> 1.33 us
    slice x1 -> x0, local copies, waits for them, and re-layouts: 0.58 us -> none  [local(): pairing = plan[0] + plan[1] - 15]
where the time goes in v3:
time: 47.2 us; the launch traced here: 47 us
  Pallas kernels  43.4 us (92%)
  local copies, waits for them, and re-layouts  1.96 us (4%)
  between operations  0.71 us (2%)
  other arithmetic  0.63 us (1%)
    pallas_call x1, Pallas kernels, call(): pl.pallas_call(functools.partial(kernel, pairing), out_shape=jax.ShapeDty...  43.4 us
    unnamed x9, local copies, waits for them, and re-layouts  1.33 us

profile of v3, /device:TPU:1, one launch (start us, length us, event | category | flops | bytes accessed | tf_op | source)
XLA Modules:
  0.0 47.0 jit_solution(1589889637258860149)
XLA Ops:
  0.0 0.0 copy-start.1
  0.0 0.0 copy-start
  0.0 0.0 copy-start.3
  0.0 0.7 %copy-done.3 = s32[2]{0:T(128)S(1)} copy-done((s32[2]{0:T(128)S(1)}, s32[2]{0:T(128)}, u32[]{:S(2)}) %copy-start.3) | copy-done | bytes 32
  0.7 0.6 %reduce_min.9 = s32[]{:T(128)} reduce(s32[2]{0:T(128)S(1)} %copy-done.3, s32[]{:T(128)} %constant.1.clone.1), dimensions={0}, to_apply=%region_0.0 | reduce | flops 1 | bytes 16 | tf_op jit(solution)/shard_map/reduce_min | solution.py:294
  1.3 0.0 copy-start.2
  2.0 0.0 copy-done.1
  2.0 0.0 copy-done
  2.0 0.0 copy-done.2
  2.0 44.4 %conditional.1 = (f32[16,1024]{1,0:T(8,128)S(1)}) conditional(s32[]{:T(128)} %clamp.3, f32[16,1024]{1,0:T(8,128)S(1)} %copy-done, (f32[8]{0:T(128)S(1)}, f32[8,1024]{1,0:T(8,128)S(1)}, f32[16,1024]{1,0:T(8,128)S(1)}) %tuple.110, (f32[8]{0:T(128)S(1)}, f32[8,1024]{1,0:T(8,128)S(1)}, ...), branch_computations={%region_1.0_spmd, %region_2.0_spmd, %region_3.0_spmd, %region_4.0_... | conditional | bytes 131080 | solution.py:294
  2.1 0.6 %copy.79.vectors_ref = f32[16,1024]{1,0:T(8,128)} copy(f32[16,1024]{1,0:T(8,128)S(1)} %get-tuple-element.98) | data formatting | bytes 131072 | tf_op jit(solution)/shard_map/cond
  2.7 43.4 %branch_1_fun.1 = f32[16,1024]{1,0:T(8,128)S(1)} custom-call(f32[8]{0:T(128)S(1)} %get-tuple-element.177.scales_ref, f32[8,1024]{1,0:T(8,128)S(1)} %get-tuple-element.191.points_ref, f32[16,1024]{1,0:T(8,128)} %copy.79.vectors_ref), custom_call_target="tpu_custom_call" | custom-call | tf_op jit(solution)/shard_map/cond/branch_1_fun/pallas_call | solution.py:264
  46.4 0.6 %copy.94 = f32[16,1024]{1,0:T(8,128)} copy(f32[16,1024]{1,0:T(8,128)S(1)} %get-tuple-element.148) | data formatting | bytes 131072
Async XLA Ops:
  0.0 2.0 %copy-start.1 = (f32[8,1024]{1,0:T(8,128)S(1)}, f32[8,1024]{1,0:T(8,128)}, u32[]{:S(2)}) copy-start(f32[8,1024]{1,0:T(8,128)} %param.19) | copy-start | bytes 98308
  0.0 2.0 %copy-start = (f32[16,1024]{1,0:T(8,128)S(1)}, f32[16,1024]{1,0:T(8,128)}, u32[]{:S(2)}) copy-start(f32[16,1024]{1,0:T(8,128)} %param.21) | copy-start | bytes 196612
  0.0 0.7 %copy-start.3 = (s32[2]{0:T(128)S(1)}, s32[2]{0:T(128)}, u32[]{:S(2)}) copy-start(s32[2]{0:T(128)} %param.22) | copy-start | bytes 28
  1.3 0.7 %copy-start.2 = (f32[8]{0:T(128)S(1)}, f32[8]{0:T(128)}, u32[]{:S(2)}) copy-start(f32[8]{0:T(128)} %param.20) | copy-start | bytes 100

commit v4 on v3

--- a/solution.py
+++ b/solution.py
@@ -22,7 +22,7 @@
 CHUNK = 256
 HOPS = 4
 ORDER = ((0, 0), (0, 1), (2, 0), (2, 1), (2, 2), (2, 3), (0, 3), (0, 4), (1, 3), (1, 2), (1, 1), (1, 0), (0, 2))
-SENDS = {1: -1, 5: -1, 0: -1, 2: -1, 3: -1, 4: -1}
+SENDS = (1, 5, 0, 2, 3, 4)
 
 
 def tile_id(offset):
@@ -118,14 +118,22 @@
     back,
     sends,
     recvs,
+    locals_sem,
 ):
-    size = points_ref.shape[1]
+    size = own.shape[1]
     halves = size // UNIT
     far_team, near_team = team_id(15), team_id(pairing)
     me = lax.axis_index("team")
-    own[0:COORDS, :] = points_ref[...]
-    own[COORDS : COORDS + RHS, :] = vectors_ref[...]
+    loads = [
+        pltpu.make_async_copy(points_ref, own.at[0:COORDS], locals_sem.at[0]),
+        pltpu.make_async_copy(vectors_ref, own.at[COORDS : COORDS + RHS], locals_sem.at[1]),
+    ]
+    for load in loads:
+        load.start()
     greet([tile_id(step) for step in range(1, lax.axis_size("tile"))] + [far_team, near_team])
+
+    for load in loads:
+        load.wait()
 
     def fetch(slot):
         target = tile_id(-1 - slot) if slot < HOPS else (far_team if slot == HOPS else near_team)
@@ -140,8 +148,7 @@
         return remote(src, back.at[slot], sends.at[6 + slot], recvs.at[6 + slot], target)
 
     for slot in SENDS:
-        if SENDS[slot] < 0:
-            fetch(slot).start()
+        fetch(slot).start()
 
     line = lax.broadcasted_iota(jnp.int32, (COORDS, 1), 0)
     scales = jnp.zeros((COORDS, 1), F32)
@@ -149,15 +156,17 @@
         scales = jnp.where(line == coord, scales_ref[coord], scales)
 
     def ready_row(shard, row):
-        row_x[row * size : (row + 1) * size, :] = row_operand(shard, scales).astype(BF16)
-        row_v[:, row * size : (row + 1) * size] = shard[COORDS:].astype(BF16)
+        at = pl.ds(pl.multiple_of(row * size, size), size)
+        row_x[at, :] = row_operand(shard, scales).astype(BF16)
+        row_v[:, at] = shard[COORDS:].astype(BF16)
 
     def ready_col(shard, hop):
-        col_x[:, hop * size : (hop + 1) * size] = col_operand(shard, scales)
-        col_v[:, hop * size : (hop + 1) * size] = shard[COORDS:].astype(BF16)
-
-    ready_row(own[...], 0)
-    ready_col(own[...], 0)
+        at = pl.ds(pl.multiple_of(hop * size, size), size)
+        col_x[:, at] = col_operand(shard, scales)
+        col_v[:, at] = shard[COORDS:].astype(BF16)
+
+    ready_row(own[...], jnp.int32(0))
+    ready_col(own[...], jnp.int32(0))
     acc_r[...] = jnp.zeros_like(acc_r)
     acc_c[...] = jnp.zeros_like(acc_c)
     upper = (lax.axis_index("tile") >= lax.axis_size("tile") // 2).astype(jnp.int32)
@@ -172,6 +181,13 @@
             if slot >= 0:
                 first_use.setdefault(slot, start)
                 last_use[slot] = start + count - 1
+
+    for kind in (range(HOPS), range(HOPS, HOPS + 2)):
+        taken = set()
+        for slot in sorted(kind, key=lambda slot: -first_use[slot]):
+            while first_use[slot] in taken:
+                first_use[slot] -= 1
+            taken.add(first_use[slot])
 
     def where(unit):
         shard, place, index = jnp.int32(0), jnp.int32(0), unit
@@ -204,23 +220,22 @@
 
     def step(unit, carry):
         for number in range(units):
-            leaving = [slot for slot in SENDS if SENDS[slot] == number]
-            coming = [slot for slot in first_use if first_use[slot] == number + 1]
             giving = [slot for slot in last_use if last_use[slot] == number - 2]
-            if leaving or coming or giving:
+            if giving:
 
                 @pl.when(unit == number)
-                def _(leaving=leaving, coming=coming, giving=giving):
-                    for slot in leaving:
-                        fetch(slot).start()
+                def _(giving=giving):
                     for slot in giving:
                         give(slot).start()
-                    for slot in coming:
-                        fetch(slot).wait_recv()
-                        if slot < HOPS:
-                            ready_col(came[slot], slot + 1)
-                        else:
-                            ready_row(came[slot], slot - 3)
+
+        for slots, ready in ((range(HOPS), ready_col), (range(HOPS, HOPS + 2), ready_row)):
+            due = [(slot, first_use[slot] - 1) for slot in slots]
+
+            @pl.when(functools.reduce(jnp.logical_or, [unit == number for _, number in due]))
+            def _(due=due, ready=ready, shift=1 if ready is ready_col else 1 - HOPS):
+                slot = sum(jnp.where(unit == number, slot, 0) for slot, number in due)
+                remote(own, came.at[slot], sends.at[slot], recvs.at[slot], far_team).wait_recv()
+                ready(came[slot], slot + shift)
 
         last, current, following = carry
         for at in range(0, UNIT, CHUNK):
@@ -243,7 +258,7 @@
     for slot in last_use:
         if last_use[slot] > units - 3:
             give(slot).start()
-    total = 0.5 * vectors_ref[...] + acc_r[:, 0:size] + acc_c[:, 0:size]
+    total = 0.5 * own[COORDS : COORDS + RHS, :] + acc_r[:, 0:size] + acc_c[:, 0:size]
     for slot in sorted(last_use, key=lambda slot: last_use[slot]):
         give(slot).wait_recv()
         total = total + back[slot]
@@ -264,7 +279,7 @@
         return pl.pallas_call(
             functools.partial(kernel, pairing),
             out_shape=jax.ShapeDtypeStruct((RHS, size), F32),
-            in_specs=[pl.BlockSpec(memory_space=pltpu.SMEM)] + vmem(2),
+            in_specs=[pl.BlockSpec(memory_space=pltpu.SMEM)] + [pl.BlockSpec(memory_space=pl.ANY)] * 2,
             out_specs=vmem(1)[0],
             scratch_shapes=[
                 VMEM((COORDS + RHS, size), F32),
@@ -280,6 +295,7 @@
                 VMEM((6, RHS, size), F32),
                 dma((12,)),
                 dma((12,)),
+                dma((2,)),
             ],
             compiler_params=pltpu.CompilerParams(
                 collective_id=pairing - 1, has_side_effects=True, vmem_limit_bytes=60 << 20
@@ -291,7 +307,7 @@
 
 def local(points, scales, vectors, plan):
     kernels = [paired(number) for number in range(1, 15)]
-    return lax.switch(jnp.min(plan), [lambda scales, points, vectors: vectors] + kernels, scales, points, vectors)
+    return lax.switch(jnp.min(plan), [lambda *args: jnp.zeros(vectors.shape, F32)] + kernels, scales, points, vectors)
 
 
 def solution(mesh):

time: 47.2 us -> 45.5 us (0.964)
  Pallas kernels: 43.4 us -> 42.4 us
  local copies, waits for them, and re-layouts: 1.96 us -> 1.29 us
    pallas_call x1, Pallas kernels: 43.4 us -> 42.4 us  [call(): pl.pallas_call(functools.partial(kernel, pairing), out_shape=jax.ShapeDty...]
    cond x1 -> x0, local copies, waits for them, and re-layouts: 0.63 us -> none
    unnamed x9 -> x5, local copies, waits for them, and re-layouts: 1.33 us -> 1.29 us
where the time goes in v4:
time: 45.5 us; the launch traced here: 45.4 us
  Pallas kernels  42.4 us (93%)
  local copies, waits for them, and re-layouts  1.29 us (3%)
  between operations  0.69 us (2%)
  other arithmetic  0.63 us (1%)
    pallas_call x1, Pallas kernels, call(): pl.pallas_call(functools.partial(kernel, pairing), out_shape=jax.ShapeDty...  42.4 us
    unnamed x5, local copies, waits for them, and re-layouts  1.29 us

profile of v4, /device:TPU:1, one launch (start us, length us, event | category | flops | bytes accessed | tf_op | source)
XLA Modules:
  0.0 45.4 jit_solution(10547113869317813302)
XLA Ops:
  0.0 0.0 copy-start.1
  0.0 0.7 %copy-done.1 = s32[2]{0:T(128)S(1)} copy-done((s32[2]{0:T(128)S(1)}, s32[2]{0:T(128)}, u32[]{:S(2)}) %copy-start.1) | copy-done | bytes 32
  0.7 0.6 %reduce_min.9 = s32[]{:T(128)} reduce(s32[2]{0:T(128)S(1)} %copy-done.1, s32[]{:T(128)} %constant.2.clone.1), dimensions={0}, to_apply=%region_0.0 | reduce | flops 1 | bytes 16 | tf_op jit(solution)/shard_map/reduce_min | solution.py:310
  1.3 0.0 copy-start
  2.0 0.0 copy-done
  2.0 42.7 %conditional.1 = (f32[16,1024]{1,0:T(8,128)S(1)}) conditional(s32[]{:T(128)} %clamp.3, () %tuple.50, (f32[8]{0:T(128)S(1)}, f32[8,1024]{1,0:T(8,128)}, f32[16,1024]{1,0:T(8,128)}) %tuple.82, (f32[8]{0:T(128)S(1)}, f32[8,1024]{1,0:T(8,128)}, f32[16,1024]{1,0:T(8,128)}) %tuple.83, (f32[8]{0:T(128)S(1)}, ...), branch_computations={%region_1.0_spmd, %region_2.0_spmd, %region_3.0_spmd, %region_4.0_... | conditional | bytes 65548 | solution.py:310
  2.0 42.4 %branch_5_fun.1 = f32[16,1024]{1,0:T(8,128)S(1)} custom-call(f32[8]{0:T(128)S(1)} %get-tuple-element.194.scales_ref, f32[8,1024]{1,0:T(8,128)} %get-tuple-element.208.points_ref, f32[16,1024]{1,0:T(8,128)} %get-tuple-element.222.vectors_ref), custom_call_target="tpu_custom_call" | custom-call | tf_op jit(solution)/shard_map/cond/branch_5_fun/pallas_call | solution.py:279
  44.7 0.6 %copy.78 = f32[16,1024]{1,0:T(8,128)} copy(f32[16,1024]{1,0:T(8,128)S(1)} %get-tuple-element.147) | data formatting | bytes 131072
Async XLA Ops:
  0.0 0.7 %copy-start.1 = (s32[2]{0:T(128)S(1)}, s32[2]{0:T(128)}, u32[]{:S(2)}) copy-start(s32[2]{0:T(128)} %param.22) | copy-start | bytes 28
  1.3 0.7 %copy-start = (f32[8]{0:T(128)S(1)}, f32[8]{0:T(128)}, u32[]{:S(2)}) copy-start(f32[8]{0:T(128)} %param.20) | copy-start | bytes 100

commit v5 on v4

--- a/solution.py
+++ b/solution.py
@@ -21,8 +21,8 @@
 UNIT = 512
 CHUNK = 256
 HOPS = 4
-ORDER = ((0, 0), (0, 1), (2, 0), (2, 1), (2, 2), (2, 3), (0, 3), (0, 4), (1, 3), (1, 2), (1, 1), (1, 0), (0, 2))
-SENDS = (1, 5, 0, 2, 3, 4)
+ORDER = ((0, 0), (0, 1), (2, 0), (2, 1), (2, 2), (2, 3), (0, 3), (0, 4), (1, 2), (1, 3), (1, 1), (1, 0), (0, 2))
+SENDS = (0, 5, 1, 4, 2, 3)
 
 
 def tile_id(offset):
@@ -218,7 +218,7 @@
             col_v[:, cols], part, (((1,), (1,)), ((), ())), preferred_element_type=F32
         )
 
-    def step(unit, carry):
+    def errands(unit):
         for number in range(units):
             giving = [slot for slot in last_use if last_use[slot] == number - 2]
             if giving:
@@ -236,6 +236,18 @@
                 slot = sum(jnp.where(unit == number, slot, 0) for slot, number in due)
                 remote(own, came.at[slot], sends.at[slot], recvs.at[slot], far_team).wait_recv()
                 ready(came[slot], slot + shift)
+
+    def step(unit, carry):
+        busy = [0, 0]
+        for number in [first_use[slot] - 1 for slot in first_use] + [last_use[slot] + 2 for slot in last_use]:
+            if number < units:
+                busy[number // 32] |= 1 << number % 32
+        low, high = [jnp.int32(word - (1 << 32) if word >> 31 else word) for word in busy]
+        flags = jnp.where(unit < 32, low, high)
+
+        @pl.when(jnp.bitwise_and(lax.shift_right_logical(flags, jnp.bitwise_and(unit, 31)), 1) == 1)
+        def _():
+            errands(unit)
 
         last, current, following = carry
         for at in range(0, UNIT, CHUNK):

time: 45.5 us -> 44.1 us (0.969)
  Pallas kernels: 42.4 us -> 41 us
    pallas_call x1, Pallas kernels: 42.4 us -> 41 us  [call(): pl.pallas_call(functools.partial(kernel, pairing), out_shape=jax.ShapeDty...]
where the time goes in v5:
time: 44.1 us; the launch traced here: 44 us
  Pallas kernels  41 us (93%)
  local copies, waits for them, and re-layouts  1.29 us (3%)
  between operations  0.69 us (2%)
  other arithmetic  0.63 us (1%)
    pallas_call x1, Pallas kernels, call(): pl.pallas_call(functools.partial(kernel, pairing), out_shape=jax.ShapeDty...  41 us
    unnamed x5, local copies, waits for them, and re-layouts  1.29 us

profile of v5, /device:TPU:1, one launch (start us, length us, event | category | flops | bytes accessed | tf_op | source)
XLA Modules:
  0.0 44.0 jit_solution(10092272003584994996)
XLA Ops:
  0.0 0.0 copy-start.1
  0.0 0.7 %copy-done.1 = s32[2]{0:T(128)S(1)} copy-done((s32[2]{0:T(128)S(1)}, s32[2]{0:T(128)}, u32[]{:S(2)}) %copy-start.1) | copy-done | bytes 32
  0.7 0.6 %reduce_min.9 = s32[]{:T(128)} reduce(s32[2]{0:T(128)S(1)} %copy-done.1, s32[]{:T(128)} %constant.2.clone.1), dimensions={0}, to_apply=%region_0.0 | reduce | flops 1 | bytes 16 | tf_op jit(solution)/shard_map/reduce_min | solution.py:322
  1.3 0.0 copy-start
  2.0 0.0 copy-done
  2.0 41.4 %conditional.1 = (f32[16,1024]{1,0:T(8,128)S(1)}) conditional(s32[]{:T(128)} %clamp.3, () %tuple.50, (f32[8]{0:T(128)S(1)}, f32[8,1024]{1,0:T(8,128)}, f32[16,1024]{1,0:T(8,128)}) %tuple.82, (f32[8]{0:T(128)S(1)}, f32[8,1024]{1,0:T(8,128)}, f32[16,1024]{1,0:T(8,128)}) %tuple.83, (f32[8]{0:T(128)S(1)}, ...), branch_computations={%region_1.0_spmd, %region_2.0_spmd, %region_3.0_spmd, %region_4.0_... | conditional | bytes 65548 | solution.py:322
  2.0 41.0 %branch_4_fun.1 = f32[16,1024]{1,0:T(8,128)S(1)} custom-call(f32[8]{0:T(128)S(1)} %get-tuple-element.193.scales_ref, f32[8,1024]{1,0:T(8,128)} %get-tuple-element.207.points_ref, f32[16,1024]{1,0:T(8,128)} %get-tuple-element.221.vectors_ref), custom_call_target="tpu_custom_call" | custom-call | tf_op jit(solution)/shard_map/cond/branch_4_fun/pallas_call | solution.py:291
  43.3 0.6 %copy.78 = f32[16,1024]{1,0:T(8,128)} copy(f32[16,1024]{1,0:T(8,128)S(1)} %get-tuple-element.147) | data formatting | bytes 131072
Async XLA Ops:
  0.0 0.7 %copy-start.1 = (s32[2]{0:T(128)S(1)}, s32[2]{0:T(128)}, u32[]{:S(2)}) copy-start(s32[2]{0:T(128)} %param.22) | copy-start | bytes 28
  1.3 0.7 %copy-start = (f32[8]{0:T(128)S(1)}, f32[8]{0:T(128)}, u32[]{:S(2)}) copy-start(f32[8]{0:T(128)} %param.20) | copy-start | bytes 100

commit v6 on v5

--- a/solution.py
+++ b/solution.py
@@ -119,6 +119,7 @@
     sends,
     recvs,
     locals_sem,
+    lengths,
 ):
     size = own.shape[1]
     halves = size // UNIT
@@ -128,7 +129,8 @@
         pltpu.make_async_copy(points_ref, own.at[0:COORDS], locals_sem.at[0]),
         pltpu.make_async_copy(vectors_ref, own.at[COORDS : COORDS + RHS], locals_sem.at[1]),
     ]
-    for load in loads:
+    lengths_load = pltpu.make_async_copy(scales_ref, lengths, locals_sem.at[2])
+    for load in loads + [lengths_load]:
         load.start()
     greet([tile_id(step) for step in range(1, lax.axis_size("tile"))] + [far_team, near_team])
 
@@ -151,9 +153,10 @@
         fetch(slot).start()
 
     line = lax.broadcasted_iota(jnp.int32, (COORDS, 1), 0)
+    lengths_load.wait()
     scales = jnp.zeros((COORDS, 1), F32)
     for coord in range(COORDS):
-        scales = jnp.where(line == coord, scales_ref[coord], scales)
+        scales = jnp.where(line == coord, lengths[coord], scales)
 
     def ready_row(shard, row):
         at = pl.ds(pl.multiple_of(row * size, size), size)
@@ -291,7 +294,7 @@
         return pl.pallas_call(
             functools.partial(kernel, pairing),
             out_shape=jax.ShapeDtypeStruct((RHS, size), F32),
-            in_specs=[pl.BlockSpec(memory_space=pltpu.SMEM)] + [pl.BlockSpec(memory_space=pl.ANY)] * 2,
+            in_specs=[pl.BlockSpec(memory_space=pl.ANY)] * 3,
             out_specs=vmem(1)[0],
             scratch_shapes=[
                 VMEM((COORDS + RHS, size), F32),
@@ -307,7 +310,8 @@
                 VMEM((6, RHS, size), F32),
                 dma((12,)),
                 dma((12,)),
-                dma((2,)),
+                dma((3,)),
+                pltpu.SMEM((COORDS,), F32),
             ],
             compiler_params=pltpu.CompilerParams(
                 collective_id=pairing - 1, has_side_effects=True, vmem_limit_bytes=60 << 20

time: 44.1 us -> 45 us (1.020)
  no operation moved by 1% of the time
where the time goes in v6:
time: 45 us; the launch traced here: 44.5 us
  Pallas kernels  41.4 us (92%)
  local copies, waits for them, and re-layouts  1.29 us (3%)
  between operations  0.69 us (2%)
  other arithmetic  0.63 us (1%)
  loops' own time  0.54 us (1%)
    pallas_call x1, Pallas kernels, call(): pl.pallas_call(functools.partial(kernel, pairing), out_shape=jax.ShapeDty...  41.4 us
    unnamed x5, local copies, waits for them, and re-layouts  1.29 us

profile of v6, /device:TPU:1, one launch (start us, length us, event | category | flops | bytes accessed | tf_op | source)
XLA Modules:
  0.0 44.5 jit_solution(12254789475723744822)
XLA Ops:
  0.0 0.0 copy-start.1
  0.0 0.7 %copy-done.1 = s32[2]{0:T(128)S(1)} copy-done((s32[2]{0:T(128)S(1)}, s32[2]{0:T(128)}, u32[]{:S(2)}) %copy-start.1) | copy-done | bytes 32
  0.7 0.6 %reduce_min.9 = s32[]{:T(128)} reduce(s32[2]{0:T(128)S(1)} %copy-done.1, s32[]{:T(128)} %constant.2.clone.1), dimensions={0}, to_apply=%region_0.0 | reduce | flops 1 | bytes 16 | tf_op jit(solution)/shard_map/reduce_min | solution.py:326
  1.3 0.0 copy-start
  2.0 0.0 copy-done
  2.0 41.9 %conditional.1 = (f32[16,1024]{1,0:T(8,128)S(1)}) conditional(s32[]{:T(128)} %clamp.3, () %tuple.50, (f32[8]{0:T(128)S(1)}, f32[8,1024]{1,0:T(8,128)}, f32[16,1024]{1,0:T(8,128)}) %tuple.82, (f32[8]{0:T(128)S(1)}, f32[8,1024]{1,0:T(8,128)}, f32[16,1024]{1,0:T(8,128)}) %tuple.83, (f32[8]{0:T(128)S(1)}, ...), branch_computations={%region_1.0_spmd, %region_2.0_spmd, %region_3.0_spmd, %region_4.0_... | conditional | bytes 65548 | solution.py:326
  2.0 41.4 %branch_8_fun.1 = f32[16,1024]{1,0:T(8,128)S(1)} custom-call(f32[8]{0:T(128)S(1)} %get-tuple-element.197.scales_ref, f32[8,1024]{1,0:T(8,128)} %get-tuple-element.211.points_ref, f32[16,1024]{1,0:T(8,128)} %get-tuple-element.225.vectors_ref), custom_call_target="tpu_custom_call" | custom-call | tf_op jit(solution)/shard_map/cond/branch_8_fun/pallas_call | solution.py:294
  43.9 0.6 %copy.78 = f32[16,1024]{1,0:T(8,128)} copy(f32[16,1024]{1,0:T(8,128)S(1)} %get-tuple-element.147) | data formatting | bytes 131072
Async XLA Ops:
  0.0 0.7 %copy-start.1 = (s32[2]{0:T(128)S(1)}, s32[2]{0:T(128)}, u32[]{:S(2)}) copy-start(s32[2]{0:T(128)} %param.22) | copy-start | bytes 28
  1.3 0.7 %copy-start = (f32[8]{0:T(128)S(1)}, f32[8]{0:T(128)}, u32[]{:S(2)}) copy-start(f32[8]{0:T(128)} %param.20) | copy-start | bytes 100
